TPU v7x, 32 devices: a whole 2x2x4 slice. The times are simulated.
32 devices in a mesh: vin: 8 (over z, core), vout: 2 (over x), cell: 2 (over y).
Axes of the slice: x: 2, y: 2, z: 4, core: 2. Of those that a mesh axis runs over, the one named last changes fastest.
Arguments:
- distribution: bfloat16 [8, 13824, 4, 128], P('vout', 'vin', 'cell'), may hold values from -6 to 6
- collision: bfloat16 [13824, 13824], P('vout', 'vin'), may hold values from -1 to 3
- speeds: float32 [3, 13824], P(None, 'vout'), may hold values from 0.05 to 0.3
- directions: int32 [3, 13824], P(None, 'vout'), may hold values from 0 to 1
- cell_flags: int32 [8, 4, 128], P('vin', 'cell'), may hold values 0 or 1
Outputs:
- updated: bfloat16 [8, 13824, 4, 128], P('vin', 'vout', 'cell')
Inputs may be any that keep to these rules, and one draw needn't show every extreme that they name: `directions`: 1 means the component is positive, 0 negative. `cell_flags`: 1 marks a solid cell, where nothing is transported.
All inputs are finite; a program needn't handle non-finite values. No bound on the sum of `cell_flags` on one device may be relied on, other than what follows from the above.
Results may differ from a plain program's by a relative error of at most 0.023.
Values may be sent and summed in bfloat16 or wider, within the bound.
A program may use at most 128 MiB of HBM per device.

v0:
```python
import jax
import jax.numpy as jnp
from jax import lax
from jax.sharding import PartitionSpec as P

CHUNKS = 3
CORES = 2


def from_lower(values, axis):
    ends = lax.axis_size(axis) - 1
    return lax.ppermute(values, axis, [(i, i + 1) for i in range(ends)])


def from_higher(values, axis):
    ends = lax.axis_size(axis) - 1
    return lax.ppermute(values, axis, [(i + 1, i) for i in range(ends)])


def hop(values, axis, pairs):
    return lax.ppermute(values, axis, pairs)


def core_pairs(axis):
    return [(i, i + 1 - 2 * (i % CORES)) for i in range(lax.axis_size(axis))]


def scatter_line(own, axis):
    chips = lax.axis_size(axis) // CORES
    chip = lax.axis_index(axis) // CORES
    total = lax.dynamic_index_in_dim(own, chip, 0, keepdims=False).astype(jnp.float32)
    up = down = None
    for step in range(chips - 1):
        target = jnp.clip(chips - 1 - step + chip, 0, chips - 1)
        lower = jnp.clip(step - (chips - 1 - chip), 0, chips - 1)
        send_up = lax.dynamic_index_in_dim(own, target, 0, keepdims=False)
        send_down = lax.dynamic_index_in_dim(own, lower, 0, keepdims=False)
        if step:
            send_up = (send_up.astype(jnp.float32) + up.astype(jnp.float32)).astype(own.dtype)
            send_down = (send_down.astype(jnp.float32) + down.astype(jnp.float32)).astype(own.dtype)
        rising, falling = ([], [])
        for at in range(step + 1):
            mirror = chips - 1 - at
            for core in range(CORES):
                rising.append((at * CORES + core, (at + 1) * CORES + core))
                falling.append((mirror * CORES + core, (mirror - 1) * CORES + core))
        up = hop(send_up, axis, rising)
        down = hop(send_down, axis, falling)
    if up is not None:
        total = total + up.astype(jnp.float32) + down.astype(jnp.float32)
    return total.astype(own.dtype)


def shifted(values, step):
    edge = jnp.zeros_like(values[..., :1])
    if step > 0:
        return jnp.concatenate([edge, values[..., :-1]], axis=-1)
    return jnp.concatenate([values[..., 1:], edge], axis=-1)


def transport(center, neighbours, speeds, positive, fluid):
    middle = center.astype(jnp.float32)
    flux = jnp.zeros_like(middle)
    for component, (low, high) in enumerate(neighbours):
        upstream = jnp.where(positive[component][:, None, None], low, high).astype(jnp.float32)
        flux = flux + speeds[component][:, None, None] * (middle - upstream)
    return (middle - fluid[None] * flux).astype(jnp.bfloat16)


def on_device(distribution, collision, speeds, directions, cell_flags):
    velocities = collision.shape[0]
    chunk = velocities // CHUNKS
    planes = lax.all_gather(distribution, "vout", axis=0, tiled=True)
    planes = planes.reshape((planes.shape[0] // CORES, CORES) + planes.shape[1:])
    core = lax.rem(lax.axis_index("vin"), CORES)
    mine = lax.dynamic_index_in_dim(planes, core, 1, keepdims=False)
    theirs = lax.dynamic_index_in_dim(planes, 1 - core, 1, keepdims=False)
    fluid = (1 - cell_flags[0]).astype(jnp.float32)
    outs = []
    for part in range(CHUNKS):
        own = slice(part * chunk, (part + 1) * chunk)
        block = collision[own]
        spec = "vu,zuyx->zvyx"
        away = jnp.einsum(spec, block, theirs, preferred_element_type=jnp.float32)
        near = jnp.einsum(spec, block, mine, preferred_element_type=jnp.float32)
        got = hop(away.astype(jnp.bfloat16), "vin", core_pairs("vin"))
        both = (near + got.astype(jnp.float32)).astype(jnp.bfloat16)
        cells = scatter_line(both, "vin")
        before = from_lower(cells[:, -1:], "cell")
        after = from_higher(cells[:, :1], "cell")
        neighbours = (
            (shifted(cells, 1), shifted(cells, -1)),
            (
                jnp.concatenate([before, cells[:, :-1]], axis=1),
                jnp.concatenate([cells[:, 1:], after], axis=1),
            ),
            (from_lower(cells, "vin"), from_higher(cells, "vin")),
        )
        outs.append(transport(cells, neighbours, speeds[:, own], directions[:, own] == 1, fluid))
    return jnp.concatenate(outs, axis=0)[None]


def solution(mesh):
    return jax.shard_map(
        on_device,
        mesh=mesh,
        in_specs=(
            P("vout", "vin", "cell", None),
            P("vout", "vin"),
            P(None, "vout"),
            P(None, "vout"),
            P("vin", "cell", None),
        ),
        out_specs=P("vin", "vout", "cell", None),
        check_vma=False,
    )
```

profile of v0, /device:TPU:8, one launch (start us, length us, event | category | flops | bytes accessed | tf_op | source)
XLA Modules:
  0.0 504.9 jit_solution(819726647843778147)
XLA Ops:
  6.5 4.2 copy.9
  10.8 90.5 %all-gather.2.cloned.1.call-done = bf16[8,1728,2,128]{3,1,2,0:T(8,128)(2,1)} async-done(((bf16[4,1728,2,128]{3,1,2,0:T(8,128)(2,1)}), bf16[8,1728,2,128]{3,1,2,0:T(8,128)(2,1)}) %all-gather.2.cloned.1.call-update) | async-done | bytes 7077904 | tf_op jit(solution)/shard_map/all_gather | solution.py:73
  101.4 14.5 %fusion.42 = bf16[4,2304,2,128]{1,3,2,0:T(8,128)(2,1)} fusion(bf16[6912,1728]{0,1:T(8,128)(2,1)} %param.6, bf16[4,2,1728,2,128]{4,2,3,1,0:T(8,128)(2,1)} %bitcast.137, s32[]{:T(128)S(6)} %select_n.67), kind=kOutput, calls=%fused_computation.29 | convolution fusion | flops 8156086272 | bytes 16220164 | tf_op jit(solution)/shard_map/vu,zuyx->zvyx/dot_general | solution.py:84
  115.9 13.7 %fusion.39 = bf16[4,2304,2,128]{1,3,2,0:T(8,128)(2,1)} fusion(bf16[6912,1728]{0,1:T(8,128)(2,1)} %param.6, bf16[4,2,1728,2,128]{4,2,3,1,0:T(8,128)(2,1)S(1)} %bitcast.141, s32[]{:T(128)S(6)} %select_n.67), kind=kOutput, calls=%fused_computation.28 | convolution fusion | flops 8156086272 | bytes 16220164 | tf_op jit(solution)/shard_map/vu,zuyx->zvyx/dot_general | solution.py:84
  130.1 14.2 %fusion.36 = bf16[4,2304,2,128]{1,3,2,0:T(8,128)(2,1)} fusion(bf16[6912,1728]{0,1:T(8,128)(2,1)} %param.6, bf16[4,2,1728,2,128]{4,2,3,1,0:T(8,128)(2,1)S(1)} %bitcast.142, s32[]{:T(128)S(6)} %select_n.67), kind=kOutput, calls=%fused_computation.27 | convolution fusion | flops 8156086272 | bytes 16220164 | tf_op jit(solution)/shard_map/vu,zuyx->zvyx/dot_general | solution.py:84
  145.0 13.6 %fusion.2 = bf16[4,2304,2,128]{1,3,2,0:T(8,128)(2,1)S(1)} fusion(bf16[4,2304,2,128]{1,3,2,0:T(8,128)(2,1)} %collective-permute-done, bf16[6912,1728]{0,1:T(8,128)(2,1)} %param.6, bf16[4,2,1728,2,128]{4,2,3,1,0:T(8,128)(2,1)} %bitcast.138, s32[]{:T(128)S(6)} %select_n.66), kind=kOutput, calls=%fused_computation.5 | convolution fusion | flops 8160804864 | bytes 20938756 | tf_op jit(solution)/shard_map/vu,zuyx->zvyx/dot_general | solution.py:85
  161.7 13.7 %fusion.1 = bf16[4,2304,2,128]{1,3,2,0:T(8,128)(2,1)S(1)} fusion(bf16[4,2304,2,128]{1,3,2,0:T(8,128)(2,1)} %collective-permute-done.11, bf16[6912,1728]{0,1:T(8,128)(2,1)} %param.6, bf16[4,2,1728,2,128]{4,2,3,1,0:T(8,128)(2,1)} %bitcast.139, s32[]{:T(128)S(6)} %select_n.66), kind=kOutput, calls=%fused_computation.3 | convolution fusion | flops 8160804864 | bytes 20938756 | tf_op jit(solution)/shard_map/vu,zuyx->zvyx/dot_general | solution.py:85
  178.6 13.6 %fusion = bf16[4,2304,2,128]{1,3,2,0:T(8,128)(2,1)S(1)} fusion(bf16[4,2304,2,128]{1,3,2,0:T(8,128)(2,1)} %collective-permute-done.22, bf16[6912,1728]{0,1:T(8,128)(2,1)} %param.6, bf16[4,2,1728,2,128]{4,2,3,1,0:T(8,128)(2,1)} %bitcast.140, s32[]{:T(128)S(6)} %select_n.66), kind=kOutput, calls=%fused_computation.1 | convolution fusion | flops 8160804864 | bytes 20938756 | tf_op jit(solution)/shard_map/vu,zuyx->zvyx/dot_general | solution.py:85
  194.7 20.1 %collective-permute-done.12 = bf16[2304,2,128]{0,2,1:T(8,128)(2,1)} collective-permute-done((bf16[2304,2,128]{0,2,1:T(8,128)(2,1)S(1)}, bf16[2304,2,128]{0,2,1:T(8,128)(2,1)}, u32[]{:S(2)}, u32[]{:S(2)}) %collective-permute-start.12) | collective-permute-done | bytes 1179680 | tf_op jit(solution)/shard_map/ppermute | solution.py:21
  218.3 21.7 %collective-permute-done.23 = bf16[2304,2,128]{0,2,1:T(8,128)(2,1)S(1)} collective-permute-done((bf16[2304,2,128]{0,2,1:T(8,128)(2,1)S(1)}, bf16[2304,2,128]{0,2,1:T(8,128)(2,1)S(1)}, u32[]{:S(2)}, u32[]{:S(2)}) %collective-permute-start.23) | collective-permute-done | bytes 1179680 | tf_op jit(solution)/shard_map/ppermute | solution.py:21
  244.1 21.1 %collective-permute-done.2 = bf16[2304,2,128]{0,2,1:T(8,128)(2,1)S(1)} collective-permute-done((bf16[2304,2,128]{0,2,1:T(8,128)(2,1)S(1)}, bf16[2304,2,128]{0,2,1:T(8,128)(2,1)S(1)}, u32[]{:S(2)}, u32[]{:S(2)}) %collective-permute-start.2) | collective-permute-done | bytes 1179680 | tf_op jit(solution)/shard_map/ppermute | solution.py:21
  268.4 4.8 collective-permute-start.3
  273.2 17.3 %collective-permute-done.13 = bf16[2304,2,128]{0,2,1:T(8,128)(2,1)S(1)} collective-permute-done((bf16[2304,2,128]{0,2,1:T(8,128)(2,1)S(1)}, bf16[2304,2,128]{0,2,1:T(8,128)(2,1)S(1)}, u32[]{:S(2)}, u32[]{:S(2)}) %collective-permute-start.13) | collective-permute-done | bytes 1179680 | tf_op jit(solution)/shard_map/ppermute | solution.py:21
  293.7 4.6 collective-permute-start.14
  298.2 17.5 %collective-permute-done.24 = bf16[2304,2,128]{0,2,1:T(8,128)(2,1)S(1)} collective-permute-done((bf16[2304,2,128]{0,2,1:T(8,128)(2,1)S(1)}, bf16[2304,2,128]{0,2,1:T(8,128)(2,1)S(1)}, u32[]{:S(2)}, u32[]{:S(2)}) %collective-permute-start.24) | collective-permute-done | bytes 1179680 | tf_op jit(solution)/shard_map/ppermute | solution.py:21
  317.7 4.6 collective-permute-start.25
  324.9 23.0 %collective-permute-done.27 = bf16[2304,2,128]{0,2,1:T(8,128)(2,1)S(1)} collective-permute-done((bf16[2304,2,128]{0,2,1:T(8,128)(2,1)S(1)}, bf16[2304,2,128]{0,2,1:T(8,128)(2,1)S(1)}, u32[]{:S(2)}, u32[]{:S(2)}) %collective-permute-start.27) | collective-permute-done | bytes 1179680 | tf_op jit(solution)/shard_map/ppermute | solution.py:21
  352.0 21.1 %collective-permute-done.6 = bf16[2304,2,128]{0,2,1:T(8,128)(2,1)S(1)} collective-permute-done((bf16[2304,2,128]{0,2,1:T(8,128)(2,1)S(1)}, bf16[2304,2,128]{0,2,1:T(8,128)(2,1)S(1)}, u32[]{:S(2)}, u32[]{:S(2)}) %collective-permute-start.6) | collective-permute-done | bytes 1179680 | tf_op jit(solution)/shard_map/ppermute | solution.py:21
  375.9 2.4 collective-permute-start.9
  378.3 20.2 %collective-permute-done.17 = bf16[2304,2,128]{0,2,1:T(8,128)(2,1)S(1)} collective-permute-done((bf16[2304,2,128]{0,2,1:T(8,128)(2,1)S(1)}, bf16[2304,2,128]{0,2,1:T(8,128)(2,1)S(1)}, u32[]{:S(2)}, u32[]{:S(2)}) %collective-permute-start.17) | collective-permute-done | bytes 1179680 | tf_op jit(solution)/shard_map/ppermute | solution.py:21
  401.2 3.4 collective-permute-start.7
  404.7 17.9 %collective-permute-done.28 = bf16[2304,2,128]{0,2,1:T(8,128)(2,1)S(1)} collective-permute-done((bf16[2304,2,128]{0,2,1:T(8,128)(2,1)S(1)}, bf16[2304,2,128]{0,2,1:T(8,128)(2,1)S(1)}, u32[]{:S(2)}, u32[]{:S(2)}) %collective-permute-start.28) | collective-permute-done | bytes 1179680 | tf_op jit(solution)/shard_map/ppermute | solution.py:21
  426.5 12.0 %collective-permute-done.8 = bf16[2304,1,128]{0,2,1:T(8,128)(2,1)S(1)} collective-permute-done((bf16[2304,1,128]{0,2,1:T(8,128)(2,1)S(1)}, bf16[2304,1,128]{0,2,1:T(8,128)(2,1)S(1)}, u32[]{:S(2)}, u32[]{:S(2)}) %collective-permute-start.8) | collective-permute-done | bytes 589856 | tf_op jit(solution)/shard_map/ppermute | solution.py:17
  440.1 10.7 %collective-permute-done.18 = bf16[2304,1,128]{0,2,1:T(8,128)(2,1)S(1)} collective-permute-done((bf16[2304,1,128]{0,2,1:T(8,128)(2,1)S(1)}, bf16[2304,1,128]{0,2,1:T(8,128)(2,1)S(1)}, u32[]{:S(2)}, u32[]{:S(2)}) %collective-permute-start.18) | collective-permute-done | bytes 589856 | tf_op jit(solution)/shard_map/ppermute | solution.py:12
  452.7 3.6 collective-permute-start.32
  457.7 2.2 fusion.63
  459.9 12.5 %collective-permute-done.19 = bf16[2304,1,128]{0,2,1:T(8,128)(2,1)S(1)} collective-permute-done((bf16[2304,1,128]{0,2,1:T(8,128)(2,1)S(1)}, bf16[2304,1,128]{0,2,1:T(8,128)(2,1)S(1)}, u32[]{:S(2)}, u32[]{:S(2)}) %collective-permute-start.19) | collective-permute-done | bytes 589856 | tf_op jit(solution)/shard_map/ppermute | solution.py:17
  475.2 2.2 fusion.70
  477.4 7.3 %collective-permute-done.29 = bf16[2304,1,128]{0,2,1:T(8,128)(2,1)S(1)} collective-permute-done((bf16[2304,1,128]{0,2,1:T(8,128)(2,1)S(1)}, bf16[2304,1,128]{0,2,1:T(8,128)(2,1)S(1)}, u32[]{:S(2)}, u32[]{:S(2)}) %collective-permute-start.29) | collective-permute-done | bytes 589856 | tf_op jit(solution)/shard_map/ppermute | solution.py:12
  484.7 4.2 collective-permute-done.30
  488.8 2.2 fusion.77
  491.3 6.5 %copy.12 = bf16[1,6912,2,128]{3,2,1,0:T(2,128)(2,1)} copy(bf16[1,6912,2,128]{1,3,2,0:T(8,128)(2,1)S(1)} %maximum_bitcast_fusion) | data formatting | bytes 7077888 | tf_op jit(solution)/shard_map/broadcast_in_dim | solution.py:100
  (84 shorter events, 49.6 us)
Async XLA Ops:
  6.5 94.8 %all-gather.2.cloned.1.call-start = ((), (), s32[]{:S(2)}) async-start(), calls=%async_computation | async-start | bytes 10616832 | tf_op jit(solution)/shard_map/all_gather | solution.py:73
  115.8 29.1 %collective-permute-start = (bf16[4,2304,2,128]{1,3,2,0:T(8,128)(2,1)}, bf16[4,2304,2,128]{1,3,2,0:T(8,128)(2,1)}, u32[]{:S(2)}, u32[]{:S(2)}) collective-permute-start(bf16[4,2304,2,128]{1,3,2,0:T(8,128)(2,1)} %fusion.42), channel_id=1, source_target_pairs={{0,4},{4,0},{8,12},{12,8},{16,20},{20,16},{24,28},{28,24},{1,5},{5... | collective-permute-start | bytes 14155784 | tf_op jit(solution)/shard_map/ppermute | solution.py:21
  129.6 32.1 %collective-permute-start.11 = (bf16[4,2304,2,128]{1,3,2,0:T(8,128)(2,1)}, bf16[4,2304,2,128]{1,3,2,0:T(8,128)(2,1)}, u32[]{:S(2)}, u32[]{:S(2)}) collective-permute-start(bf16[4,2304,2,128]{1,3,2,0:T(8,128)(2,1)} %fusion.39), channel_id=1, source_target_pairs={{0,4},{4,0},{8,12},{12,8},{16,20},{20,16},{24,28},{28,24},{1,5},{5... | collective-permute-start | bytes 14155784 | tf_op jit(solution)/shard_map/ppermute | solution.py:21
  144.3 34.3 %collective-permute-start.22 = (bf16[4,2304,2,128]{1,3,2,0:T(8,128)(2,1)}, bf16[4,2304,2,128]{1,3,2,0:T(8,128)(2,1)}, u32[]{:S(2)}, u32[]{:S(2)}) collective-permute-start(bf16[4,2304,2,128]{1,3,2,0:T(8,128)(2,1)} %fusion.36), channel_id=1, source_target_pairs={{0,4},{4,0},{8,12},{12,8},{16,20},{20,16},{24,28},{28,24},{1,5},{5... | collective-permute-start | bytes 14155784 | tf_op jit(solution)/shard_map/ppermute | solution.py:21
  158.7 34.9 %collective-permute-start.1 = (bf16[2304,2,128]{0,2,1:T(8,128)(2,1)S(1)}, bf16[2304,2,128]{0,2,1:T(8,128)(2,1)S(1)}, u32[]{:S(2)}, u32[]{:S(2)}) collective-permute-start(bf16[2304,2,128]{0,2,1:T(8,128)(2,1)S(1)} %get-tuple-element.25), channel_id=1, source_target_pairs={{0,8},{4,12},{1,9},{5,13},{2,10},{6,14},{3,11},{7,15}} | collective-permute-start | bytes 3538952 | tf_op jit(solution)/shard_map/ppermute | solution.py:21
  160.0 82.2 %collective-permute-start.4 = (bf16[2304,2,128]{0,2,1:T(8,128)(2,1)S(1)}, bf16[2304,2,128]{0,2,1:T(8,128)(2,1)}, u32[]{:S(2)}, u32[]{:S(2)}) collective-permute-start(bf16[2304,2,128]{0,2,1:T(8,128)(2,1)S(1)} %get-tuple-element.26), channel_id=1, source_target_pairs={{24,16},{28,20},{25,17},{29,21},{26,18},{30,22},{27,19},{31,23}} | collective-permute-start | bytes 3538952 | tf_op jit(solution)/shard_map/ppermute | solution.py:21
  175.6 39.2 %collective-permute-start.12 = (bf16[2304,2,128]{0,2,1:T(8,128)(2,1)S(1)}, bf16[2304,2,128]{0,2,1:T(8,128)(2,1)}, u32[]{:S(2)}, u32[]{:S(2)}) collective-permute-start(bf16[2304,2,128]{0,2,1:T(8,128)(2,1)S(1)} %get-tuple-element.29), channel_id=1, source_target_pairs={{0,8},{4,12},{1,9},{5,13},{2,10},{6,14},{3,11},{7,15}} | collective-permute-start | bytes 3538952 | tf_op jit(solution)/shard_map/ppermute | solution.py:21
  176.9 91.5 %collective-permute-start.15 = (bf16[2304,2,128]{0,2,1:T(8,128)(2,1)S(1)}, bf16[2304,2,128]{0,2,1:T(8,128)(2,1)}, u32[]{:S(2)}, u32[]{:S(2)}) collective-permute-start(bf16[2304,2,128]{0,2,1:T(8,128)(2,1)S(1)} %get-tuple-element.30), channel_id=1, source_target_pairs={{24,16},{28,20},{25,17},{29,21},{26,18},{30,22},{27,19},{31,23}} | collective-permute-start | bytes 3538952 | tf_op jit(solution)/shard_map/ppermute | solution.py:21
  192.3 47.6 %collective-permute-start.23 = (bf16[2304,2,128]{0,2,1:T(8,128)(2,1)S(1)}, bf16[2304,2,128]{0,2,1:T(8,128)(2,1)S(1)}, u32[]{:S(2)}, u32[]{:S(2)}) collective-permute-start(bf16[2304,2,128]{0,2,1:T(8,128)(2,1)S(1)} %get-tuple-element.33), channel_id=1, source_target_pairs={{0,8},{4,12},{1,9},{5,13},{2,10},{6,14},{3,11},{7,15}} | collective-permute-start | bytes 3538952 | tf_op jit(solution)/shard_map/ppermute | solution.py:21
  193.6 100.0 %collective-permute-start.26 = (bf16[2304,2,128]{0,2,1:T(8,128)(2,1)S(1)}, bf16[2304,2,128]{0,2,1:T(8,128)(2,1)S(1)}, u32[]{:S(2)}, u32[]{:S(2)}) collective-permute-start(bf16[2304,2,128]{0,2,1:T(8,128)(2,1)S(1)} %get-tuple-element.34), channel_id=1, source_target_pairs={{24,16},{28,20},{25,17},{29,21},{26,18},{30,22},{27,19},{31,23}} | collective-permute-start | bytes 3538952 | tf_op jit(solution)/shard_map/ppermute | solution.py:21
  214.8 50.5 %collective-permute-start.2 = (bf16[2304,2,128]{0,2,1:T(8,128)(2,1)S(1)}, bf16[2304,2,128]{0,2,1:T(8,128)(2,1)S(1)}, u32[]{:S(2)}, u32[]{:S(2)}) collective-permute-start(bf16[2304,2,128]{0,2,1:T(8,128)(2,1)S(1)} %fusion.92), channel_id=1, source_target_pairs={{0,8},{4,12},{8,16},{12,20},{1,9},{5,13},{9,17},{13,21},{2,10},{6,... | collective-permute-start | bytes 3538952 | tf_op jit(solution)/shard_map/ppermute | solution.py:21
  239.9 50.6 %collective-permute-start.13 = (bf16[2304,2,128]{0,2,1:T(8,128)(2,1)S(1)}, bf16[2304,2,128]{0,2,1:T(8,128)(2,1)S(1)}, u32[]{:S(2)}, u32[]{:S(2)}) collective-permute-start(bf16[2304,2,128]{0,2,1:T(8,128)(2,1)S(1)} %fusion.86), channel_id=1, source_target_pairs={{0,8},{4,12},{8,16},{12,20},{1,9},{5,13},{9,17},{13,21},{2,10},{6,... | collective-permute-start | bytes 3538952 | tf_op jit(solution)/shard_map/ppermute | solution.py:21
  242.2 73.6 %collective-permute-start.24 = (bf16[2304,2,128]{0,2,1:T(8,128)(2,1)S(1)}, bf16[2304,2,128]{0,2,1:T(8,128)(2,1)S(1)}, u32[]{:S(2)}, u32[]{:S(2)}) collective-permute-start(bf16[2304,2,128]{0,2,1:T(8,128)(2,1)S(1)} %fusion.80), channel_id=1, source_target_pairs={{0,8},{4,12},{8,16},{12,20},{1,9},{5,13},{9,17},{13,21},{2,10},{6,... | collective-permute-start | bytes 3538952 | tf_op jit(solution)/shard_map/ppermute | solution.py:21
  267.1 50.6 %collective-permute-start.5 = (bf16[2304,2,128]{0,2,1:T(8,128)(2,1)S(1)}, bf16[2304,2,128]{0,2,1:T(8,128)(2,1)S(1)}, u32[]{:S(2)}, u32[]{:S(2)}) collective-permute-start(bf16[2304,2,128]{0,2,1:T(8,128)(2,1)S(1)} %get-tuple-element.24), channel_id=1, source_target_pairs={{24,16},{28,20},{16,8},{20,12},{25,17},{29,21},{17,9},{21,13},{26,... | collective-permute-start | bytes 3538952 | tf_op jit(solution)/shard_map/ppermute | solution.py:21
  268.4 81.7 %collective-permute-start.3 = (bf16[2304,2,128]{0,2,1:T(8,128)(2,1)S(1)}, bf16[2304,2,128]{0,2,1:T(8,128)(2,1)S(1)}, u32[]{:S(2)}, u32[]{:S(2)}) collective-permute-start(bf16[2304,2,128]{0,2,1:T(8,128)(2,1)S(1)} %get-tuple-element.23), channel_id=1, source_target_pairs={{0,8},{4,12},{8,16},{12,20},{16,24},{20,28},{1,9},{5,13},{9,17},{1... | collective-permute-start | bytes 3538952 | tf_op jit(solution)/shard_map/ppermute | solution.py:21
  292.4 30.2 %collective-permute-start.16 = (bf16[2304,2,128]{0,2,1:T(8,128)(2,1)S(1)}, bf16[2304,2,128]{0,2,1:T(8,128)(2,1)S(1)}, u32[]{:S(2)}, u32[]{:S(2)}) collective-permute-start(bf16[2304,2,128]{0,2,1:T(8,128)(2,1)S(1)} %get-tuple-element.28), channel_id=1, source_target_pairs={{24,16},{28,20},{16,8},{20,12},{25,17},{29,21},{17,9},{21,13},{26,... | collective-permute-start | bytes 3538952 | tf_op jit(solution)/shard_map/ppermute | solution.py:21
  293.7 82.2 %collective-permute-start.14 = (bf16[2304,2,128]{0,2,1:T(8,128)(2,1)S(1)}, bf16[2304,2,128]{0,2,1:T(8,128)(2,1)S(1)}, u32[]{:S(2)}, u32[]{:S(2)}) collective-permute-start(bf16[2304,2,128]{0,2,1:T(8,128)(2,1)S(1)} %get-tuple-element.27), channel_id=1, source_target_pairs={{0,8},{4,12},{8,16},{12,20},{16,24},{20,28},{1,9},{5,13},{9,17},{1... | collective-permute-start | bytes 3538952 | tf_op jit(solution)/shard_map/ppermute | solution.py:21
  316.4 31.5 %collective-permute-start.27 = (bf16[2304,2,128]{0,2,1:T(8,128)(2,1)S(1)}, bf16[2304,2,128]{0,2,1:T(8,128)(2,1)S(1)}, u32[]{:S(2)}, u32[]{:S(2)}) collective-permute-start(bf16[2304,2,128]{0,2,1:T(8,128)(2,1)S(1)} %get-tuple-element.32), channel_id=1, source_target_pairs={{24,16},{28,20},{16,8},{20,12},{25,17},{29,21},{17,9},{21,13},{26,... | collective-permute-start | bytes 3538952 | tf_op jit(solution)/shard_map/ppermute | solution.py:21
  317.7 83.6 %collective-permute-start.25 = (bf16[2304,2,128]{0,2,1:T(8,128)(2,1)S(1)}, bf16[2304,2,128]{0,2,1:T(8,128)(2,1)S(1)}, u32[]{:S(2)}, u32[]{:S(2)}) collective-permute-start(bf16[2304,2,128]{0,2,1:T(8,128)(2,1)S(1)} %get-tuple-element.31), channel_id=1, source_target_pairs={{0,8},{4,12},{8,16},{12,20},{16,24},{20,28},{1,9},{5,13},{9,17},{1... | collective-permute-start | bytes 3538952 | tf_op jit(solution)/shard_map/ppermute | solution.py:21
  322.6 50.6 %collective-permute-start.6 = (bf16[2304,2,128]{0,2,1:T(8,128)(2,1)S(1)}, bf16[2304,2,128]{0,2,1:T(8,128)(2,1)S(1)}, u32[]{:S(2)}, u32[]{:S(2)}) collective-permute-start(bf16[2304,2,128]{0,2,1:T(8,128)(2,1)S(1)} %fusion.91), channel_id=1, source_target_pairs={{24,16},{28,20},{16,8},{20,12},{8,0},{12,4},{25,17},{29,21},{17,9}... | collective-permute-start | bytes 3538952 | tf_op jit(solution)/shard_map/ppermute | solution.py:21
  347.9 50.6 %collective-permute-start.17 = (bf16[2304,2,128]{0,2,1:T(8,128)(2,1)S(1)}, bf16[2304,2,128]{0,2,1:T(8,128)(2,1)S(1)}, u32[]{:S(2)}, u32[]{:S(2)}) collective-permute-start(bf16[2304,2,128]{0,2,1:T(8,128)(2,1)S(1)} %fusion.85), channel_id=1, source_target_pairs={{24,16},{28,20},{16,8},{20,12},{8,0},{12,4},{25,17},{29,21},{17,9}... | collective-permute-start | bytes 3538952 | tf_op jit(solution)/shard_map/ppermute | solution.py:21
  350.1 72.4 %collective-permute-start.28 = (bf16[2304,2,128]{0,2,1:T(8,128)(2,1)S(1)}, bf16[2304,2,128]{0,2,1:T(8,128)(2,1)S(1)}, u32[]{:S(2)}, u32[]{:S(2)}) collective-permute-start(bf16[2304,2,128]{0,2,1:T(8,128)(2,1)S(1)} %fusion.79), channel_id=1, source_target_pairs={{24,16},{28,20},{16,8},{20,12},{8,0},{12,4},{25,17},{29,21},{17,9}... | collective-permute-start | bytes 3538952 | tf_op jit(solution)/shard_map/ppermute | solution.py:21
  373.6 79.0 %collective-permute-start.10 = (bf16[2304,2,128]{0,2,1:T(8,128)(2,1)S(1)}, bf16[2304,2,128]{0,2,1:T(8,128)(2,1)S(1)}, u32[]{:S(2)}, u32[]{:S(2)}) collective-permute-start(bf16[2304,2,128]{0,2,1:T(8,128)(2,1)S(1)} %fusion.95), channel_id=1, source_target_pairs={{4,0},{8,4},{12,8},{16,12},{20,16},{24,20},{28,24},{5,1},{9,5},{13... | collective-permute-start | bytes 3538952 | tf_op jit(solution)/shard_map/ppermute | solution.py:17
  375.9 80.5 %collective-permute-start.9 = (bf16[2304,2,128]{0,2,1:T(8,128)(2,1)S(1)}, bf16[2304,2,128]{0,2,1:T(8,128)(2,1)S(1)}, u32[]{:S(2)}, u32[]{:S(2)}) collective-permute-start(bf16[2304,2,128]{0,2,1:T(8,128)(2,1)S(1)} %fusion.95), channel_id=1, source_target_pairs={{0,4},{4,8},{8,12},{12,16},{16,20},{20,24},{24,28},{1,5},{5,9},{9,... | collective-permute-start | bytes 3538952 | tf_op jit(solution)/shard_map/ppermute | solution.py:12
  398.9 74.9 %collective-permute-start.20 = (bf16[2304,2,128]{0,2,1:T(8,128)(2,1)S(1)}, bf16[2304,2,128]{0,2,1:T(8,128)(2,1)S(1)}, u32[]{:S(2)}, u32[]{:S(2)}) collective-permute-start(bf16[2304,2,128]{0,2,1:T(8,128)(2,1)S(1)} %fusion.89), channel_id=1, source_target_pairs={{0,4},{4,8},{8,12},{12,16},{16,20},{20,24},{24,28},{1,5},{5,9},{9,... | collective-permute-start | bytes 3538952 | tf_op jit(solution)/shard_map/ppermute | solution.py:12
  401.2 23.4 %collective-permute-start.7 = (bf16[2304,1,128]{0,2,1:T(8,128)(2,1)S(1)}, bf16[2304,1,128]{0,2,1:T(8,128)(2,1)S(1)}, u32[]{:S(2)}, u32[]{:S(2)}) collective-permute-start(bf16[2304,1,128]{0,2,1:T(8,128)(2,1)S(1)} %get-tuple-element.37), channel_id=1, source_target_pairs={{0,1},{2,3},{4,5},{6,7},{8,9},{10,11},{12,13},{14,15},{16,17},{18,... | collective-permute-start | bytes 1769480 | tf_op jit(solution)/shard_map/ppermute | solution.py:12
  422.5 16.0 %collective-permute-start.8 = (bf16[2304,1,128]{0,2,1:T(8,128)(2,1)S(1)}, bf16[2304,1,128]{0,2,1:T(8,128)(2,1)S(1)}, u32[]{:S(2)}, u32[]{:S(2)}) collective-permute-start(bf16[2304,1,128]{0,2,1:T(8,128)(2,1)S(1)} %get-tuple-element.38), channel_id=1, source_target_pairs={{1,0},{3,2},{5,4},{7,6},{9,8},{11,10},{13,12},{15,14},{17,16},{19,... | collective-permute-start | bytes 1769480 | tf_op jit(solution)/shard_map/ppermute | solution.py:17
  424.6 50.6 %collective-permute-start.21 = (bf16[2304,2,128]{0,2,1:T(8,128)(2,1)S(1)}, bf16[2304,2,128]{0,2,1:T(8,128)(2,1)S(1)}, u32[]{:S(2)}, u32[]{:S(2)}) collective-permute-start(bf16[2304,2,128]{0,2,1:T(8,128)(2,1)S(1)} %fusion.89), channel_id=1, source_target_pairs={{4,0},{8,4},{12,8},{16,12},{20,16},{24,20},{28,24},{5,1},{9,5},{13... | collective-permute-start | bytes 3538952 | tf_op jit(solution)/shard_map/ppermute | solution.py:17
  450.8 38.1 %collective-permute-start.31 = (bf16[2304,2,128]{0,2,1:T(8,128)(2,1)S(1)}, bf16[2304,2,128]{0,2,1:T(8,128)(2,1)S(1)}, u32[]{:S(2)}, u32[]{:S(2)}) collective-permute-start(bf16[2304,2,128]{0,2,1:T(8,128)(2,1)S(1)} %fusion.83), channel_id=1, source_target_pairs={{0,4},{4,8},{8,12},{12,16},{16,20},{20,24},{24,28},{1,5},{5,9},{9,... | collective-permute-start | bytes 3538952 | tf_op jit(solution)/shard_map/ppermute | solution.py:12
  452.7 36.1 %collective-permute-start.32 = (bf16[2304,2,128]{0,2,1:T(8,128)(2,1)S(1)}, bf16[2304,2,128]{0,2,1:T(8,128)(2,1)S(1)}, u32[]{:S(2)}, u32[]{:S(2)}) collective-permute-start(bf16[2304,2,128]{0,2,1:T(8,128)(2,1)S(1)} %fusion.83), channel_id=1, source_target_pairs={{4,0},{8,4},{12,8},{16,12},{20,16},{24,20},{28,24},{5,1},{9,5},{13... | collective-permute-start | bytes 3538952 | tf_op jit(solution)/shard_map/ppermute | solution.py:17
  456.4 16.0 %collective-permute-start.19 = (bf16[2304,1,128]{0,2,1:T(8,128)(2,1)S(1)}, bf16[2304,1,128]{0,2,1:T(8,128)(2,1)S(1)}, u32[]{:S(2)}, u32[]{:S(2)}) collective-permute-start(bf16[2304,1,128]{0,2,1:T(8,128)(2,1)S(1)} %get-tuple-element.42), channel_id=1, source_target_pairs={{1,0},{3,2},{5,4},{7,6},{9,8},{11,10},{13,12},{15,14},{17,16},{19,... | collective-permute-start | bytes 1769480 | tf_op jit(solution)/shard_map/ppermute | solution.py:17
  473.9 14.9 %collective-permute-start.30 = (bf16[2304,1,128]{0,2,1:T(8,128)(2,1)S(1)}, bf16[2304,1,128]{0,2,1:T(8,128)(2,1)S(1)}, u32[]{:S(2)}, u32[]{:S(2)}) collective-permute-start(bf16[2304,1,128]{0,2,1:T(8,128)(2,1)S(1)} %get-tuple-element.46), channel_id=1, source_target_pairs={{1,0},{3,2},{5,4},{7,6},{9,8},{11,10},{13,12},{15,14},{17,16},{19,... | collective-permute-start | bytes 1769480 | tf_op jit(solution)/shard_map/ppermute | solution.py:17
  (6 other events, 84.2 us)
Sparse Core Ops, SparseCore 0:
  10.9 90.3 all-gather.1
where the time goes:
time: 513 us; the launch traced here: 505 us
  waiting for transfers between devices  317 us (62%)
  matrix products  83.3 us (16%)
  starting transfers between devices  61.7 us (12%)
  other arithmetic  15.7 us (3%)
  between operations  14.2 us (3%)
  local copies, waits for them, and re-layouts  12.8 us (2%)
    ppermute x21, waiting for transfers between devices, hop(): return lax.ppermute(values, axis, pairs)  180 us
    all_gather x1, waiting for transfers between devices, on_device(): planes = lax.all_gather(distribution, 'vout', axis=0, tiled=True)  90.5 us
    dot_general x3, matrix products, on_device(): away = jnp.einsum(spec, block, theirs, preferred_element_type=jnp.float32)  42.4 us
    dot_general x3, matrix products, on_device(): near = jnp.einsum(spec, block, mine, preferred_element_type=jnp.float32)  40.9 us
    ppermute x21, starting transfers between devices, hop(): return lax.ppermute(values, axis, pairs)  37.7 us
    ppermute x6, waiting for transfers between devices, from_higher(): return lax.ppermute(values, axis, [(i + 1, i) for i in range(ends)])  28.7 us
    ppermute x6, waiting for transfers between devices, from_lower(): return lax.ppermute(values, axis, [(i, i + 1) for i in range(ends)])  18 us
    ppermute x6, starting transfers between devices, from_lower(): return lax.ppermute(values, axis, [(i, i + 1) for i in range(ends)])  12.6 us
  transfers between devices with their start and end apart: 34, of which 16 were waited for; matrix products, arithmetic and copies ran while one was open for 17% of the time, Pallas kernels for 0%

commit v1 on v0

--- a/solution.py
+++ b/solution.py
@@ -5,6 +5,18 @@
 
 CHUNKS = 3
 CORES = 2
+
+
+def gather_by_bits(x, axis, dim):
+    ways, here, lap = (lax.axis_size(axis), lax.axis_index(axis), x.shape[dim])
+    line, have = (x, 1)
+    while have < ways:
+        line = jnp.concatenate(
+            [line, lax.ppermute(line, axis, [(d, (d - have) % ways) for d in range(ways)])],
+            axis=dim,
+        )
+        have = 2 * have
+    return jnp.roll(line, here * lap, axis=dim)
 
 
 def from_lower(values, axis):
@@ -70,7 +82,7 @@
 def on_device(distribution, collision, speeds, directions, cell_flags):
     velocities = collision.shape[0]
     chunk = velocities // CHUNKS
-    planes = lax.all_gather(distribution, "vout", axis=0, tiled=True)
+    planes = gather_by_bits(distribution, "vout", 0)
     planes = planes.reshape((planes.shape[0] // CORES, CORES) + planes.shape[1:])
     core = lax.rem(lax.axis_index("vin"), CORES)
     mine = lax.dynamic_index_in_dim(planes, core, 1, keepdims=False)

time: 513 us -> 494 us (0.963)
  waiting for transfers between devices: 317 us -> 302 us
  between operations: 14.2 us -> 0.84 us
  other arithmetic: 15.7 us -> 21.7 us
    all_gather x1 -> x0, waiting for transfers between devices: 90.5 us -> none  [on_device(): planes = lax.all_gather(distribution, 'vout', axis=0, tiled=True)]
    ppermute x0 -> x1, waiting for transfers between devices: none -> 76.9 us  [gather_by_bits(): lax.ppermute(line, axis, [(d, (d - have) % ways) for d in range(ways)])]
    concatenate x0 -> x1, other arithmetic: none -> 6.04 us  [gather_by_bits(): return jnp.roll(line, here * lap, axis=dim)]
where the time goes in v1:
time: 494 us; the launch traced here: 485 us
  waiting for transfers between devices  302 us (61%)
  matrix products  85 us (17%)
  starting transfers between devices  64.5 us (13%)
  other arithmetic  21.7 us (4%)
  local copies, waits for them, and re-layouts  11 us (2%)
    ppermute x21, waiting for transfers between devices, hop(): return lax.ppermute(values, axis, pairs)  179 us
    ppermute x1, waiting for transfers between devices, gather_by_bits(): lax.ppermute(line, axis, [(d, (d - have) % ways) for d in range(ways)])  76.9 us
    dot_general x3, matrix products, on_device(): away = jnp.einsum(spec, block, theirs, preferred_element_type=jnp.float32)  44.2 us
    dot_general x3, matrix products, on_device(): near = jnp.einsum(spec, block, mine, preferred_element_type=jnp.float32)  40.9 us
    ppermute x21, starting transfers between devices, hop(): return lax.ppermute(values, axis, pairs)  37.7 us
    ppermute x6, waiting for transfers between devices, from_higher(): return lax.ppermute(values, axis, [(i + 1, i) for i in range(ends)])  28.6 us
    ppermute x6, waiting for transfers between devices, from_lower(): return lax.ppermute(values, axis, [(i, i + 1) for i in range(ends)])  18 us
    ppermute x6, starting transfers between devices, from_higher(): return lax.ppermute(values, axis, [(i + 1, i) for i in range(ends)])  13.1 us
  transfers between devices with their start and end apart: 34, of which 16 were waited for; matrix products, arithmetic and copies ran while one was open for 17% of the time, Pallas kernels for 0%

profile of v1, /device:TPU:8, one launch (start us, length us, event | category | flops | bytes accessed | tf_op | source)
XLA Modules:
  0.0 485.4 jit_solution(18411083895661937374)
XLA Ops:
  0.0 2.5 copy.8
  4.0 76.9 %collective-permute-done = bf16[4,1728,2,128]{3,1,2,0:T(8,128)(2,1)} collective-permute-done((bf16[4,1728,2,128]{3,1,2,0:T(8,128)(2,1)S(1)}, bf16[4,1728,2,128]{3,1,2,0:T(8,128)(2,1)}, u32[]{:S(2)}, u32[]{:S(2)}) %collective-permute-start) | collective-permute-done | bytes 3538976 | tf_op jit(solution)/shard_map/ppermute | solution.py:15
  80.9 6.0 %fusion.17 = bf16[8,1728,2,128]{3,1,2,0:T(8,128)(2,1)S(1)} fusion(s32[]{:T(128)S(6)} %select_n.79, bf16[4,1728,2,128]{3,1,2,0:T(8,128)(2,1)S(1)} %copy.8, bf16[4,1728,2,128]{3,1,2,0:T(8,128)(2,1)} %collective-permute-done), kind=kLoop, calls=%fused_computation.24 | loop fusion | flops 10616832 | bytes 14155780 | tf_op jit(solution)/shard_map/jit(_roll_dynamic)/concatenate | solution.py:19
  87.0 16.4 %fusion.45 = bf16[4,2304,2,128]{1,3,2,0:T(8,128)(2,1)} fusion(bf16[6912,1728]{0,1:T(8,128)(2,1)} %param.6, bf16[4,2,1728,2,128]{4,2,3,1,0:T(8,128)(2,1)S(1)} %bitcast.133, s32[]{:T(128)S(6)} %select_n.81), kind=kOutput, calls=%fused_computation.36 | convolution fusion | flops 8156086272 | bytes 16220164 | tf_op jit(solution)/shard_map/vu,zuyx->zvyx/dot_general | solution.py:96
  103.3 13.7 %fusion.42 = bf16[4,2304,2,128]{1,3,2,0:T(8,128)(2,1)} fusion(bf16[6912,1728]{0,1:T(8,128)(2,1)} %param.6, bf16[4,2,1728,2,128]{4,2,3,1,0:T(8,128)(2,1)S(1)} %bitcast.134, s32[]{:T(128)S(6)} %select_n.81), kind=kOutput, calls=%fused_computation.35 | convolution fusion | flops 8156086272 | bytes 16220164 | tf_op jit(solution)/shard_map/vu,zuyx->zvyx/dot_general | solution.py:96
  117.5 14.1 %fusion.39 = bf16[4,2304,2,128]{1,3,2,0:T(8,128)(2,1)} fusion(bf16[6912,1728]{0,1:T(8,128)(2,1)} %param.6, bf16[4,2,1728,2,128]{4,2,3,1,0:T(8,128)(2,1)S(1)} %bitcast.135, s32[]{:T(128)S(6)} %select_n.81), kind=kOutput, calls=%fused_computation.34 | convolution fusion | flops 8156086272 | bytes 16220164 | tf_op jit(solution)/shard_map/vu,zuyx->zvyx/dot_general | solution.py:96
  132.3 13.6 %fusion.2 = bf16[4,2304,2,128]{1,3,2,0:T(8,128)(2,1)S(1)} fusion(bf16[4,2304,2,128]{1,3,2,0:T(8,128)(2,1)} %collective-permute-done.1, bf16[6912,1728]{0,1:T(8,128)(2,1)} %param.6, bf16[4,2,1728,2,128]{4,2,3,1,0:T(8,128)(2,1)} %bitcast.136, s32[]{:T(128)S(6)} %select_n.80), kind=kOutput, calls=%fused_computation.9 | convolution fusion | flops 8160804864 | bytes 20938756 | tf_op jit(solution)/shard_map/vu,zuyx->zvyx/dot_general | solution.py:97
  149.0 13.7 %fusion.1 = bf16[4,2304,2,128]{1,3,2,0:T(8,128)(2,1)S(1)} fusion(bf16[4,2304,2,128]{1,3,2,0:T(8,128)(2,1)} %collective-permute-done.12, bf16[6912,1728]{0,1:T(8,128)(2,1)} %param.6, bf16[4,2,1728,2,128]{4,2,3,1,0:T(8,128)(2,1)} %bitcast.137, s32[]{:T(128)S(6)} %select_n.80), kind=kOutput, calls=%fused_computation.7 | convolution fusion | flops 8160804864 | bytes 20938756 | tf_op jit(solution)/shard_map/vu,zuyx->zvyx/dot_general | solution.py:97
  165.9 13.6 %fusion = bf16[4,2304,2,128]{1,3,2,0:T(8,128)(2,1)S(1)} fusion(bf16[4,2304,2,128]{1,3,2,0:T(8,128)(2,1)} %collective-permute-done.23, bf16[6912,1728]{0,1:T(8,128)(2,1)} %param.6, bf16[4,2,1728,2,128]{4,2,3,1,0:T(8,128)(2,1)} %bitcast.138, s32[]{:T(128)S(6)} %select_n.80), kind=kOutput, calls=%fused_computation.5 | convolution fusion | flops 8160804864 | bytes 20938756 | tf_op jit(solution)/shard_map/vu,zuyx->zvyx/dot_general | solution.py:97
  182.0 20.1 %collective-permute-done.13 = bf16[2304,2,128]{0,2,1:T(8,128)(2,1)} collective-permute-done((bf16[2304,2,128]{0,2,1:T(8,128)(2,1)S(1)}, bf16[2304,2,128]{0,2,1:T(8,128)(2,1)}, u32[]{:S(2)}, u32[]{:S(2)}) %collective-permute-start.13) | collective-permute-done | bytes 1179680 | tf_op jit(solution)/shard_map/ppermute | solution.py:33
  205.6 21.7 %collective-permute-done.24 = bf16[2304,2,128]{0,2,1:T(8,128)(2,1)S(1)} collective-permute-done((bf16[2304,2,128]{0,2,1:T(8,128)(2,1)S(1)}, bf16[2304,2,128]{0,2,1:T(8,128)(2,1)S(1)}, u32[]{:S(2)}, u32[]{:S(2)}) %collective-permute-start.24) | collective-permute-done | bytes 1179680 | tf_op jit(solution)/shard_map/ppermute | solution.py:33
  231.5 21.1 %collective-permute-done.3 = bf16[2304,2,128]{0,2,1:T(8,128)(2,1)S(1)} collective-permute-done((bf16[2304,2,128]{0,2,1:T(8,128)(2,1)S(1)}, bf16[2304,2,128]{0,2,1:T(8,128)(2,1)S(1)}, u32[]{:S(2)}, u32[]{:S(2)}) %collective-permute-start.3) | collective-permute-done | bytes 1179680 | tf_op jit(solution)/shard_map/ppermute | solution.py:33
  255.8 4.8 collective-permute-start.4
  260.6 17.3 %collective-permute-done.14 = bf16[2304,2,128]{0,2,1:T(8,128)(2,1)S(1)} collective-permute-done((bf16[2304,2,128]{0,2,1:T(8,128)(2,1)S(1)}, bf16[2304,2,128]{0,2,1:T(8,128)(2,1)S(1)}, u32[]{:S(2)}, u32[]{:S(2)}) %collective-permute-start.14) | collective-permute-done | bytes 1179680 | tf_op jit(solution)/shard_map/ppermute | solution.py:33
  281.0 4.6 collective-permute-start.15
  285.6 17.5 %collective-permute-done.25 = bf16[2304,2,128]{0,2,1:T(8,128)(2,1)S(1)} collective-permute-done((bf16[2304,2,128]{0,2,1:T(8,128)(2,1)S(1)}, bf16[2304,2,128]{0,2,1:T(8,128)(2,1)S(1)}, u32[]{:S(2)}, u32[]{:S(2)}) %collective-permute-start.25) | collective-permute-done | bytes 1179680 | tf_op jit(solution)/shard_map/ppermute | solution.py:33
  305.0 4.6 collective-permute-start.26
  312.2 23.0 %collective-permute-done.28 = bf16[2304,2,128]{0,2,1:T(8,128)(2,1)S(1)} collective-permute-done((bf16[2304,2,128]{0,2,1:T(8,128)(2,1)S(1)}, bf16[2304,2,128]{0,2,1:T(8,128)(2,1)S(1)}, u32[]{:S(2)}, u32[]{:S(2)}) %collective-permute-start.28) | collective-permute-done | bytes 1179680 | tf_op jit(solution)/shard_map/ppermute | solution.py:33
  339.4 21.1 %collective-permute-done.7 = bf16[2304,2,128]{0,2,1:T(8,128)(2,1)S(1)} collective-permute-done((bf16[2304,2,128]{0,2,1:T(8,128)(2,1)S(1)}, bf16[2304,2,128]{0,2,1:T(8,128)(2,1)S(1)}, u32[]{:S(2)}, u32[]{:S(2)}) %collective-permute-start.7) | collective-permute-done | bytes 1179680 | tf_op jit(solution)/shard_map/ppermute | solution.py:33
  363.3 3.6 collective-permute-start.11
  366.9 18.9 %collective-permute-done.18 = bf16[2304,2,128]{0,2,1:T(8,128)(2,1)S(1)} collective-permute-done((bf16[2304,2,128]{0,2,1:T(8,128)(2,1)S(1)}, bf16[2304,2,128]{0,2,1:T(8,128)(2,1)S(1)}, u32[]{:S(2)}, u32[]{:S(2)}) %collective-permute-start.18) | collective-permute-done | bytes 1179680 | tf_op jit(solution)/shard_map/ppermute | solution.py:33
  388.6 3.5 collective-permute-start.8
  392.1 17.8 %collective-permute-done.29 = bf16[2304,2,128]{0,2,1:T(8,128)(2,1)S(1)} collective-permute-done((bf16[2304,2,128]{0,2,1:T(8,128)(2,1)S(1)}, bf16[2304,2,128]{0,2,1:T(8,128)(2,1)S(1)}, u32[]{:S(2)}, u32[]{:S(2)}) %collective-permute-start.29) | collective-permute-done | bytes 1179680 | tf_op jit(solution)/shard_map/ppermute | solution.py:33
  413.9 11.9 %collective-permute-done.9 = bf16[2304,1,128]{0,2,1:T(8,128)(2,1)S(1)} collective-permute-done((bf16[2304,1,128]{0,2,1:T(8,128)(2,1)S(1)}, bf16[2304,1,128]{0,2,1:T(8,128)(2,1)S(1)}, u32[]{:S(2)}, u32[]{:S(2)}) %collective-permute-start.9) | collective-permute-done | bytes 589856 | tf_op jit(solution)/shard_map/ppermute | solution.py:29
  427.4 10.7 %collective-permute-done.19 = bf16[2304,1,128]{0,2,1:T(8,128)(2,1)S(1)} collective-permute-done((bf16[2304,1,128]{0,2,1:T(8,128)(2,1)S(1)}, bf16[2304,1,128]{0,2,1:T(8,128)(2,1)S(1)}, u32[]{:S(2)}, u32[]{:S(2)}) %collective-permute-start.19) | collective-permute-done | bytes 589856 | tf_op jit(solution)/shard_map/ppermute | solution.py:24
  440.0 3.6 collective-permute-start.33
  445.0 2.2 fusion.66
  447.2 12.5 %collective-permute-done.20 = bf16[2304,1,128]{0,2,1:T(8,128)(2,1)S(1)} collective-permute-done((bf16[2304,1,128]{0,2,1:T(8,128)(2,1)S(1)}, bf16[2304,1,128]{0,2,1:T(8,128)(2,1)S(1)}, u32[]{:S(2)}, u32[]{:S(2)}) %collective-permute-start.20) | collective-permute-done | bytes 589856 | tf_op jit(solution)/shard_map/ppermute | solution.py:29
  462.5 2.2 fusion.73
  464.7 7.3 %collective-permute-done.30 = bf16[2304,1,128]{0,2,1:T(8,128)(2,1)S(1)} collective-permute-done((bf16[2304,1,128]{0,2,1:T(8,128)(2,1)S(1)}, bf16[2304,1,128]{0,2,1:T(8,128)(2,1)S(1)}, u32[]{:S(2)}, u32[]{:S(2)}) %collective-permute-start.30) | collective-permute-done | bytes 589856 | tf_op jit(solution)/shard_map/ppermute | solution.py:24
  472.0 4.2 collective-permute-done.31
  478.6 6.5 %copy.10 = bf16[1,6912,2,128]{3,2,1,0:T(2,128)(2,1)} copy(bf16[1,6912,2,128]{1,3,2,0:T(8,128)(2,1)S(1)} %maximum_bitcast_fusion) | data formatting | bytes 7077888 | tf_op jit(solution)/shard_map/broadcast_in_dim | solution.py:112
  (84 shorter events, 53.4 us)
Async XLA Ops:
  2.5 78.4 %collective-permute-start = (bf16[4,1728,2,128]{3,1,2,0:T(8,128)(2,1)S(1)}, bf16[4,1728,2,128]{3,1,2,0:T(8,128)(2,1)}, u32[]{:S(2)}, u32[]{:S(2)}) collective-permute-start(bf16[4,1728,2,128]{3,1,2,0:T(8,128)(2,1)S(1)} %copy.8), channel_id=1, source_target_pairs={{0,2},{2,0},{1,3},{3,1},{4,6},{6,4},{5,7},{7,5},{8,10},{10,8},{9,1... | collective-permute-start | bytes 10616840 | tf_op jit(solution)/shard_map/ppermute | solution.py:15
  103.3 29.0 %collective-permute-start.1 = (bf16[4,2304,2,128]{1,3,2,0:T(8,128)(2,1)}, bf16[4,2304,2,128]{1,3,2,0:T(8,128)(2,1)}, u32[]{:S(2)}, u32[]{:S(2)}) collective-permute-start(bf16[4,2304,2,128]{1,3,2,0:T(8,128)(2,1)} %fusion.45), channel_id=1, source_target_pairs={{0,4},{4,0},{8,12},{12,8},{16,20},{20,16},{24,28},{28,24},{1,5},{5... | collective-permute-start | bytes 14155784 | tf_op jit(solution)/shard_map/ppermute | solution.py:33
  117.0 32.1 %collective-permute-start.12 = (bf16[4,2304,2,128]{1,3,2,0:T(8,128)(2,1)}, bf16[4,2304,2,128]{1,3,2,0:T(8,128)(2,1)}, u32[]{:S(2)}, u32[]{:S(2)}) collective-permute-start(bf16[4,2304,2,128]{1,3,2,0:T(8,128)(2,1)} %fusion.42), channel_id=1, source_target_pairs={{0,4},{4,0},{8,12},{12,8},{16,20},{20,16},{24,28},{28,24},{1,5},{5... | collective-permute-start | bytes 14155784 | tf_op jit(solution)/shard_map/ppermute | solution.py:33
  131.6 34.3 %collective-permute-start.23 = (bf16[4,2304,2,128]{1,3,2,0:T(8,128)(2,1)}, bf16[4,2304,2,128]{1,3,2,0:T(8,128)(2,1)}, u32[]{:S(2)}, u32[]{:S(2)}) collective-permute-start(bf16[4,2304,2,128]{1,3,2,0:T(8,128)(2,1)} %fusion.39), channel_id=1, source_target_pairs={{0,4},{4,0},{8,12},{12,8},{16,20},{20,16},{24,28},{28,24},{1,5},{5... | collective-permute-start | bytes 14155784 | tf_op jit(solution)/shard_map/ppermute | solution.py:33
  146.1 34.9 %collective-permute-start.2 = (bf16[2304,2,128]{0,2,1:T(8,128)(2,1)S(1)}, bf16[2304,2,128]{0,2,1:T(8,128)(2,1)S(1)}, u32[]{:S(2)}, u32[]{:S(2)}) collective-permute-start(bf16[2304,2,128]{0,2,1:T(8,128)(2,1)S(1)} %get-tuple-element.25), channel_id=1, source_target_pairs={{0,8},{4,12},{1,9},{5,13},{2,10},{6,14},{3,11},{7,15}} | collective-permute-start | bytes 3538952 | tf_op jit(solution)/shard_map/ppermute | solution.py:33
  147.4 82.2 %collective-permute-start.5 = (bf16[2304,2,128]{0,2,1:T(8,128)(2,1)S(1)}, bf16[2304,2,128]{0,2,1:T(8,128)(2,1)}, u32[]{:S(2)}, u32[]{:S(2)}) collective-permute-start(bf16[2304,2,128]{0,2,1:T(8,128)(2,1)S(1)} %get-tuple-element.26), channel_id=1, source_target_pairs={{24,16},{28,20},{25,17},{29,21},{26,18},{30,22},{27,19},{31,23}} | collective-permute-start | bytes 3538952 | tf_op jit(solution)/shard_map/ppermute | solution.py:33
  162.9 39.2 %collective-permute-start.13 = (bf16[2304,2,128]{0,2,1:T(8,128)(2,1)S(1)}, bf16[2304,2,128]{0,2,1:T(8,128)(2,1)}, u32[]{:S(2)}, u32[]{:S(2)}) collective-permute-start(bf16[2304,2,128]{0,2,1:T(8,128)(2,1)S(1)} %get-tuple-element.29), channel_id=1, source_target_pairs={{0,8},{4,12},{1,9},{5,13},{2,10},{6,14},{3,11},{7,15}} | collective-permute-start | bytes 3538952 | tf_op jit(solution)/shard_map/ppermute | solution.py:33
  164.2 91.5 %collective-permute-start.16 = (bf16[2304,2,128]{0,2,1:T(8,128)(2,1)S(1)}, bf16[2304,2,128]{0,2,1:T(8,128)(2,1)}, u32[]{:S(2)}, u32[]{:S(2)}) collective-permute-start(bf16[2304,2,128]{0,2,1:T(8,128)(2,1)S(1)} %get-tuple-element.30), channel_id=1, source_target_pairs={{24,16},{28,20},{25,17},{29,21},{26,18},{30,22},{27,19},{31,23}} | collective-permute-start | bytes 3538952 | tf_op jit(solution)/shard_map/ppermute | solution.py:33
  179.7 47.6 %collective-permute-start.24 = (bf16[2304,2,128]{0,2,1:T(8,128)(2,1)S(1)}, bf16[2304,2,128]{0,2,1:T(8,128)(2,1)S(1)}, u32[]{:S(2)}, u32[]{:S(2)}) collective-permute-start(bf16[2304,2,128]{0,2,1:T(8,128)(2,1)S(1)} %get-tuple-element.33), channel_id=1, source_target_pairs={{0,8},{4,12},{1,9},{5,13},{2,10},{6,14},{3,11},{7,15}} | collective-permute-start | bytes 3538952 | tf_op jit(solution)/shard_map/ppermute | solution.py:33
  181.0 100.0 %collective-permute-start.27 = (bf16[2304,2,128]{0,2,1:T(8,128)(2,1)S(1)}, bf16[2304,2,128]{0,2,1:T(8,128)(2,1)S(1)}, u32[]{:S(2)}, u32[]{:S(2)}) collective-permute-start(bf16[2304,2,128]{0,2,1:T(8,128)(2,1)S(1)} %get-tuple-element.34), channel_id=1, source_target_pairs={{24,16},{28,20},{25,17},{29,21},{26,18},{30,22},{27,19},{31,23}} | collective-permute-start | bytes 3538952 | tf_op jit(solution)/shard_map/ppermute | solution.py:33
  202.1 50.5 %collective-permute-start.3 = (bf16[2304,2,128]{0,2,1:T(8,128)(2,1)S(1)}, bf16[2304,2,128]{0,2,1:T(8,128)(2,1)S(1)}, u32[]{:S(2)}, u32[]{:S(2)}) collective-permute-start(bf16[2304,2,128]{0,2,1:T(8,128)(2,1)S(1)} %fusion.95), channel_id=1, source_target_pairs={{0,8},{4,12},{8,16},{12,20},{1,9},{5,13},{9,17},{13,21},{2,10},{6,... | collective-permute-start | bytes 3538952 | tf_op jit(solution)/shard_map/ppermute | solution.py:33
  227.3 50.6 %collective-permute-start.14 = (bf16[2304,2,128]{0,2,1:T(8,128)(2,1)S(1)}, bf16[2304,2,128]{0,2,1:T(8,128)(2,1)S(1)}, u32[]{:S(2)}, u32[]{:S(2)}) collective-permute-start(bf16[2304,2,128]{0,2,1:T(8,128)(2,1)S(1)} %fusion.89), channel_id=1, source_target_pairs={{0,8},{4,12},{8,16},{12,20},{1,9},{5,13},{9,17},{13,21},{2,10},{6,... | collective-permute-start | bytes 3538952 | tf_op jit(solution)/shard_map/ppermute | solution.py:33
  229.5 73.6 %collective-permute-start.25 = (bf16[2304,2,128]{0,2,1:T(8,128)(2,1)S(1)}, bf16[2304,2,128]{0,2,1:T(8,128)(2,1)S(1)}, u32[]{:S(2)}, u32[]{:S(2)}) collective-permute-start(bf16[2304,2,128]{0,2,1:T(8,128)(2,1)S(1)} %fusion.83), channel_id=1, source_target_pairs={{0,8},{4,12},{8,16},{12,20},{1,9},{5,13},{9,17},{13,21},{2,10},{6,... | collective-permute-start | bytes 3538952 | tf_op jit(solution)/shard_map/ppermute | solution.py:33
  254.5 50.5 %collective-permute-start.6 = (bf16[2304,2,128]{0,2,1:T(8,128)(2,1)S(1)}, bf16[2304,2,128]{0,2,1:T(8,128)(2,1)S(1)}, u32[]{:S(2)}, u32[]{:S(2)}) collective-permute-start(bf16[2304,2,128]{0,2,1:T(8,128)(2,1)S(1)} %get-tuple-element.24), channel_id=1, source_target_pairs={{24,16},{28,20},{16,8},{20,12},{25,17},{29,21},{17,9},{21,13},{26,... | collective-permute-start | bytes 3538952 | tf_op jit(solution)/shard_map/ppermute | solution.py:33
  255.8 81.7 %collective-permute-start.4 = (bf16[2304,2,128]{0,2,1:T(8,128)(2,1)S(1)}, bf16[2304,2,128]{0,2,1:T(8,128)(2,1)S(1)}, u32[]{:S(2)}, u32[]{:S(2)}) collective-permute-start(bf16[2304,2,128]{0,2,1:T(8,128)(2,1)S(1)} %get-tuple-element.23), channel_id=1, source_target_pairs={{0,8},{4,12},{8,16},{12,20},{16,24},{20,28},{1,9},{5,13},{9,17},{1... | collective-permute-start | bytes 3538952 | tf_op jit(solution)/shard_map/ppermute | solution.py:33
  279.7 30.3 %collective-permute-start.17 = (bf16[2304,2,128]{0,2,1:T(8,128)(2,1)S(1)}, bf16[2304,2,128]{0,2,1:T(8,128)(2,1)S(1)}, u32[]{:S(2)}, u32[]{:S(2)}) collective-permute-start(bf16[2304,2,128]{0,2,1:T(8,128)(2,1)S(1)} %get-tuple-element.28), channel_id=1, source_target_pairs={{24,16},{28,20},{16,8},{20,12},{25,17},{29,21},{17,9},{21,13},{26,... | collective-permute-start | bytes 3538952 | tf_op jit(solution)/shard_map/ppermute | solution.py:33
  281.0 82.2 %collective-permute-start.15 = (bf16[2304,2,128]{0,2,1:T(8,128)(2,1)S(1)}, bf16[2304,2,128]{0,2,1:T(8,128)(2,1)S(1)}, u32[]{:S(2)}, u32[]{:S(2)}) collective-permute-start(bf16[2304,2,128]{0,2,1:T(8,128)(2,1)S(1)} %get-tuple-element.27), channel_id=1, source_target_pairs={{0,8},{4,12},{8,16},{12,20},{16,24},{20,28},{1,9},{5,13},{9,17},{1... | collective-permute-start | bytes 3538952 | tf_op jit(solution)/shard_map/ppermute | solution.py:33
  303.7 31.6 %collective-permute-start.28 = (bf16[2304,2,128]{0,2,1:T(8,128)(2,1)S(1)}, bf16[2304,2,128]{0,2,1:T(8,128)(2,1)S(1)}, u32[]{:S(2)}, u32[]{:S(2)}) collective-permute-start(bf16[2304,2,128]{0,2,1:T(8,128)(2,1)S(1)} %get-tuple-element.32), channel_id=1, source_target_pairs={{24,16},{28,20},{16,8},{20,12},{25,17},{29,21},{17,9},{21,13},{26,... | collective-permute-start | bytes 3538952 | tf_op jit(solution)/shard_map/ppermute | solution.py:33
  305.0 83.6 %collective-permute-start.26 = (bf16[2304,2,128]{0,2,1:T(8,128)(2,1)S(1)}, bf16[2304,2,128]{0,2,1:T(8,128)(2,1)S(1)}, u32[]{:S(2)}, u32[]{:S(2)}) collective-permute-start(bf16[2304,2,128]{0,2,1:T(8,128)(2,1)S(1)} %get-tuple-element.31), channel_id=1, source_target_pairs={{0,8},{4,12},{8,16},{12,20},{16,24},{20,28},{1,9},{5,13},{9,17},{1... | collective-permute-start | bytes 3538952 | tf_op jit(solution)/shard_map/ppermute | solution.py:33
  310.0 50.6 %collective-permute-start.7 = (bf16[2304,2,128]{0,2,1:T(8,128)(2,1)S(1)}, bf16[2304,2,128]{0,2,1:T(8,128)(2,1)S(1)}, u32[]{:S(2)}, u32[]{:S(2)}) collective-permute-start(bf16[2304,2,128]{0,2,1:T(8,128)(2,1)S(1)} %fusion.94), channel_id=1, source_target_pairs={{24,16},{28,20},{16,8},{20,12},{8,0},{12,4},{25,17},{29,21},{17,9}... | collective-permute-start | bytes 3538952 | tf_op jit(solution)/shard_map/ppermute | solution.py:33
  335.3 50.6 %collective-permute-start.18 = (bf16[2304,2,128]{0,2,1:T(8,128)(2,1)S(1)}, bf16[2304,2,128]{0,2,1:T(8,128)(2,1)S(1)}, u32[]{:S(2)}, u32[]{:S(2)}) collective-permute-start(bf16[2304,2,128]{0,2,1:T(8,128)(2,1)S(1)} %fusion.88), channel_id=1, source_target_pairs={{24,16},{28,20},{16,8},{20,12},{8,0},{12,4},{25,17},{29,21},{17,9}... | collective-permute-start | bytes 3538952 | tf_op jit(solution)/shard_map/ppermute | solution.py:33
  337.5 72.4 %collective-permute-start.29 = (bf16[2304,2,128]{0,2,1:T(8,128)(2,1)S(1)}, bf16[2304,2,128]{0,2,1:T(8,128)(2,1)S(1)}, u32[]{:S(2)}, u32[]{:S(2)}) collective-permute-start(bf16[2304,2,128]{0,2,1:T(8,128)(2,1)S(1)} %fusion.82), channel_id=1, source_target_pairs={{24,16},{28,20},{16,8},{20,12},{8,0},{12,4},{25,17},{29,21},{17,9}... | collective-permute-start | bytes 3538952 | tf_op jit(solution)/shard_map/ppermute | solution.py:33
  361.0 79.0 %collective-permute-start.10 = (bf16[2304,2,128]{0,2,1:T(8,128)(2,1)S(1)}, bf16[2304,2,128]{0,2,1:T(8,128)(2,1)S(1)}, u32[]{:S(2)}, u32[]{:S(2)}) collective-permute-start(bf16[2304,2,128]{0,2,1:T(8,128)(2,1)S(1)} %fusion.98), channel_id=1, source_target_pairs={{0,4},{4,8},{8,12},{12,16},{16,20},{20,24},{24,28},{1,5},{5,9},{9,... | collective-permute-start | bytes 3538952 | tf_op jit(solution)/shard_map/ppermute | solution.py:24
  363.3 80.4 %collective-permute-start.11 = (bf16[2304,2,128]{0,2,1:T(8,128)(2,1)S(1)}, bf16[2304,2,128]{0,2,1:T(8,128)(2,1)S(1)}, u32[]{:S(2)}, u32[]{:S(2)}) collective-permute-start(bf16[2304,2,128]{0,2,1:T(8,128)(2,1)S(1)} %fusion.98), channel_id=1, source_target_pairs={{4,0},{8,4},{12,8},{16,12},{20,16},{24,20},{28,24},{5,1},{9,5},{13... | collective-permute-start | bytes 3538952 | tf_op jit(solution)/shard_map/ppermute | solution.py:29
  386.3 74.9 %collective-permute-start.21 = (bf16[2304,2,128]{0,2,1:T(8,128)(2,1)S(1)}, bf16[2304,2,128]{0,2,1:T(8,128)(2,1)S(1)}, u32[]{:S(2)}, u32[]{:S(2)}) collective-permute-start(bf16[2304,2,128]{0,2,1:T(8,128)(2,1)S(1)} %fusion.92), channel_id=1, source_target_pairs={{0,4},{4,8},{8,12},{12,16},{16,20},{20,24},{24,28},{1,5},{5,9},{9,... | collective-permute-start | bytes 3538952 | tf_op jit(solution)/shard_map/ppermute | solution.py:24
  388.6 23.4 %collective-permute-start.8 = (bf16[2304,1,128]{0,2,1:T(8,128)(2,1)S(1)}, bf16[2304,1,128]{0,2,1:T(8,128)(2,1)S(1)}, u32[]{:S(2)}, u32[]{:S(2)}) collective-permute-start(bf16[2304,1,128]{0,2,1:T(8,128)(2,1)S(1)} %get-tuple-element.37), channel_id=1, source_target_pairs={{0,1},{2,3},{4,5},{6,7},{8,9},{10,11},{12,13},{14,15},{16,17},{18,... | collective-permute-start | bytes 1769480 | tf_op jit(solution)/shard_map/ppermute | solution.py:24
  409.9 16.0 %collective-permute-start.9 = (bf16[2304,1,128]{0,2,1:T(8,128)(2,1)S(1)}, bf16[2304,1,128]{0,2,1:T(8,128)(2,1)S(1)}, u32[]{:S(2)}, u32[]{:S(2)}) collective-permute-start(bf16[2304,1,128]{0,2,1:T(8,128)(2,1)S(1)} %get-tuple-element.38), channel_id=1, source_target_pairs={{1,0},{3,2},{5,4},{7,6},{9,8},{11,10},{13,12},{15,14},{17,16},{19,... | collective-permute-start | bytes 1769480 | tf_op jit(solution)/shard_map/ppermute | solution.py:29
  412.0 50.5 %collective-permute-start.22 = (bf16[2304,2,128]{0,2,1:T(8,128)(2,1)S(1)}, bf16[2304,2,128]{0,2,1:T(8,128)(2,1)S(1)}, u32[]{:S(2)}, u32[]{:S(2)}) collective-permute-start(bf16[2304,2,128]{0,2,1:T(8,128)(2,1)S(1)} %fusion.92), channel_id=1, source_target_pairs={{4,0},{8,4},{12,8},{16,12},{20,16},{24,20},{28,24},{5,1},{9,5},{13... | collective-permute-start | bytes 3538952 | tf_op jit(solution)/shard_map/ppermute | solution.py:29
  438.1 38.1 %collective-permute-start.32 = (bf16[2304,2,128]{0,2,1:T(8,128)(2,1)S(1)}, bf16[2304,2,128]{0,2,1:T(8,128)(2,1)S(1)}, u32[]{:S(2)}, u32[]{:S(2)}) collective-permute-start(bf16[2304,2,128]{0,2,1:T(8,128)(2,1)S(1)} %fusion.86), channel_id=1, source_target_pairs={{0,4},{4,8},{8,12},{12,16},{16,20},{20,24},{24,28},{1,5},{5,9},{9,... | collective-permute-start | bytes 3538952 | tf_op jit(solution)/shard_map/ppermute | solution.py:24
  440.0 36.1 %collective-permute-start.33 = (bf16[2304,2,128]{0,2,1:T(8,128)(2,1)S(1)}, bf16[2304,2,128]{0,2,1:T(8,128)(2,1)S(1)}, u32[]{:S(2)}, u32[]{:S(2)}) collective-permute-start(bf16[2304,2,128]{0,2,1:T(8,128)(2,1)S(1)} %fusion.86), channel_id=1, source_target_pairs={{4,0},{8,4},{12,8},{16,12},{20,16},{24,20},{28,24},{5,1},{9,5},{13... | collective-permute-start | bytes 3538952 | tf_op jit(solution)/shard_map/ppermute | solution.py:29
  443.7 16.0 %collective-permute-start.20 = (bf16[2304,1,128]{0,2,1:T(8,128)(2,1)S(1)}, bf16[2304,1,128]{0,2,1:T(8,128)(2,1)S(1)}, u32[]{:S(2)}, u32[]{:S(2)}) collective-permute-start(bf16[2304,1,128]{0,2,1:T(8,128)(2,1)S(1)} %get-tuple-element.42), channel_id=1, source_target_pairs={{1,0},{3,2},{5,4},{7,6},{9,8},{11,10},{13,12},{15,14},{17,16},{19,... | collective-permute-start | bytes 1769480 | tf_op jit(solution)/shard_map/ppermute | solution.py:29
  461.2 14.9 %collective-permute-start.31 = (bf16[2304,1,128]{0,2,1:T(8,128)(2,1)S(1)}, bf16[2304,1,128]{0,2,1:T(8,128)(2,1)S(1)}, u32[]{:S(2)}, u32[]{:S(2)}) collective-permute-start(bf16[2304,1,128]{0,2,1:T(8,128)(2,1)S(1)} %get-tuple-element.46), channel_id=1, source_target_pairs={{1,0},{3,2},{5,4},{7,6},{9,8},{11,10},{13,12},{15,14},{17,16},{19,... | collective-permute-start | bytes 1769480 | tf_op jit(solution)/shard_map/ppermute | solution.py:29
  (6 other events, 100.1 us)
